TPU v7x, 32 devices: a whole 2x2x4 slice. The times are simulated.
32 devices in a mesh: groups: 2 (over y), dp: 4 (over z), tensor: 4 (over x, core).
Axes of the slice: x: 2, y: 2, z: 4, core: 2. Of those that a mesh axis runs over, the one named last changes fastest.
Arguments:
- normed_layer_input: bfloat16 [4096, 8192], P(('groups', 'dp'), 'tensor'), parts along dimension 0, may hold values from -6 to 6
- key_value_gradient: bfloat16 [4096, 2048], P(('groups', 'dp'), 'tensor'), parts along dimension 0, may hold values from -6 to 6
- key_value_weight: bfloat16 [8192, 2048], P(None, 'tensor'), may hold values from -0.0625 to 0.0625
- adapter_down_weight: bfloat16 [8, 16, 8192], P('dp', None, 'tensor'), may hold values from -0.0625 to 0.0625
- adapter_up_weight: bfloat16 [8, 16, 2048], P('dp', None, 'tensor'), may hold values from -1.5 to 1.5
- segment_adapter: int32 [32], P(('groups', 'dp')), parts along dimension 0, may hold values from 0 to 7
- slot_per_adapter: int32 [8], replicated, may hold values from 0 to 7, each once
Outputs:
- grad_input: bfloat16 [4096, 8192], P(('groups', 'dp'), 'tensor'), parts along dimension 0
- grad_down: float32 [16, 16, 8192], P(('groups', 'dp'), None, 'tensor'), parts along dimension 0
- grad_up: float32 [16, 16, 2048], P(('groups', 'dp'), None, 'tensor'), parts along dimension 0
There are 2 independent parts, one for each index of `groups`. A program takes and returns all parts, laid end to end along the dimension named above; an argument that names none is the same for every part. Nothing has to cross between parts.
Inputs may be any that keep to these rules, and one draw needn't show every extreme that they name: `slot_per_adapter`: every slot once.
All inputs are finite; a program needn't handle non-finite values.
Results may differ from a plain program's by a relative error of at most 0.0046.
Values may be sent and summed in bfloat16 or wider, within the bound.
A program may use at most 128 MiB of HBM per device.

v0:
```python
import jax
import jax.numpy as jnp
from jax import lax
from jax.sharding import PartitionSpec as P

SEG = 128


adapter_scale = 2.0


def shards(
    normed_layer_input,
    key_value_gradient,
    key_value_weight,
    adapter_down_weight,
    adapter_up_weight,
    segment_adapter,
    slot_per_adapter,
):
    row_count, feat_count = normed_layer_input.shape
    col_count = key_value_gradient.shape[1]
    seg_count = row_count // SEG
    down_all, up_all = (
        lax.all_gather(adapter_down_weight, "dp", axis=0, tiled=True),
        lax.all_gather(adapter_up_weight, "dp", axis=0, tiled=True),
    )
    adapter_count = down_all.shape[0]
    matches = segment_adapter[:, None] == jnp.arange(adapter_count, dtype=jnp.int32)[None, :]
    chosen = jnp.sum(jnp.where(matches, slot_per_adapter[None, :], 0), axis=1)
    down_sel = down_all[chosen]
    up_sel = up_all[chosen]
    input_blocks = normed_layer_input.reshape(seg_count, SEG, feat_count)
    grad_blocks = key_value_gradient.reshape(seg_count, SEG, col_count)
    in_part = jnp.einsum("sqd,srd->sqr", input_blocks, down_sel, preferred_element_type=jnp.float32)
    grad_part = jnp.einsum("sqc,src->sqr", grad_blocks, up_sel, preferred_element_type=jnp.float32)
    low_rank_input, low_rank_gradient = lax.psum((in_part, grad_part), "tensor")
    input_scaled = (adapter_scale * low_rank_input).astype(jnp.bfloat16)
    gradient_scaled = (adapter_scale * low_rank_gradient).astype(jnp.bfloat16)
    adapter_term = jnp.einsum(
        "sqr,srd->sqd", gradient_scaled, down_sel, preferred_element_type=jnp.float32
    ).reshape(row_count, feat_count)
    partial_sum = lax.dot_general(
        key_value_gradient,
        key_value_weight,
        (((1,), (1,)), ((), ())),
        preferred_element_type=jnp.float32,
    )
    base_term = lax.psum_scatter(partial_sum, "tensor", scatter_dimension=1, tiled=True)
    grad_input = (base_term + adapter_term).astype(jnp.bfloat16)
    term_down = jnp.einsum(
        "sqr,sqd->srd", gradient_scaled, input_blocks, preferred_element_type=jnp.float32
    )
    own_up = jnp.einsum(
        "sqr,sqc->src", input_scaled, grad_blocks, preferred_element_type=jnp.float32
    )
    onehot = (chosen[None, :] == jnp.arange(adapter_count, dtype=jnp.int32)[:, None]).astype(
        jnp.float32
    )
    dense_down = jnp.einsum("as,srd->ard", onehot, term_down, precision=lax.Precision.HIGHEST)
    dense_part = jnp.einsum("as,src->arc", onehot, own_up, precision=lax.Precision.HIGHEST)
    grad_down, up_share = (
        lax.psum_scatter(dense_down, "dp", scatter_dimension=0, tiled=True),
        lax.psum_scatter(dense_part, "dp", scatter_dimension=0, tiled=True),
    )
    return (grad_input, grad_down, up_share)


def solution(mesh):
    placed = (
        P(("groups", "dp"), "tensor"),
        P(("groups", "dp"), "tensor"),
        P(None, "tensor"),
        P("dp", None, "tensor"),
        P("dp", None, "tensor"),
        P(("groups", "dp")),
        P(),
    )
    return jax.shard_map(
        shards,
        mesh=mesh,
        in_specs=placed,
        out_specs=(
            P(("groups", "dp"), "tensor"),
            P(("groups", "dp"), None, "tensor"),
            P(("groups", "dp"), None, "tensor"),
        ),
        check_vma=False,
    )
```

profile of v0, /device:TPU:0, one launch (start us, length us, event | category | flops | bytes accessed | tf_op | source)
XLA Modules:
  0.0 263.1 jit_solution(10033035412974197223)
XLA Ops:
  7.2 0.0 copy-start
  7.2 0.0 copy-start.1
  7.2 0.0 all-reduce.3.cloned.1.call-start
  7.2 17.7 %all_gather.7 = bf16[8,16,2048]{2,1,0:T(8,128)(2,1)S(1)} all-gather(bf16[2,16,2048]{2,1,0:T(8,128)(2,1)} %param.10), channel_id=1, replica_groups=mesh['groups'=2,'dp'=4,'tensor'=4] {'dp'}, dimensions={0}, use_global_device_ids=true | all-gather | bytes 655360 | tf_op jit(solution)/shard_map/all_gather | solution.py:25
  24.9 0.9 select_reduce_fusion
  25.8 14.0 %all_gather.6 = bf16[8,16,512]{2,1,0:T(8,128)(2,1)S(1)} all-gather(bf16[2,16,512]{2,1,0:T(8,128)(2,1)} %param.11), channel_id=1, replica_groups=mesh['groups'=2,'dp'=4,'tensor'=4] {'dp'}, dimensions={0}, use_global_device_ids=true | all-gather | bytes 163840 | tf_op jit(solution)/shard_map/all_gather | solution.py:26
  39.8 0.6 gather_fusion.1
  40.4 0.6 gather_fusion
  40.9 1.9 convolution_bitcast_fusion.1
  42.8 0.0 copy-done
  42.9 1.3 convolution_bitcast_fusion
  44.1 0.0 all-reduce.3.cloned.1.call-update
  44.1 0.0 reduce-scatter.4.cloned.1.call-start
  44.2 0.0 copy-done.1
  44.2 11.5 %fusion.18 = f32[512,8192]{1,0:T(8,128)} fusion(bf16[512,512]{1,0:T(8,128)(2,1)S(1)} %copy-done.1, bf16[8192,512]{1,0:T(8,128)(2,1)} %param.9), kind=kOutput, calls=%fused_computation.28 | convolution fusion | flops 4294967296 | bytes 25690112 | tf_op jit(solution)/shard_map/dot_general | solution.py:43
  55.7 0.0 reduce-scatter.4.cloned.1.call-update
  55.8 0.0 reduce-scatter.8.cloned.1.call-start
  55.8 21.1 %all-reduce.3.cloned.1.call-done = (f32[4,128,16]{1,2,0:T(8,128)}, f32[4,128,16]{1,2,0:T(8,128)}) async-done(((f32[4,128,16]{1,2,0:T(8,128)}, f32[4,128,16]{1,2,0:T(8,128)}), (f32[4,128,16]{1,2,0:T(8,128)}, f32[4,128,16]{1,2,0:T(8,128)})) %all-reduce.3.cloned.1.call-update) | async-done | bytes 65552 | tf_op jit(solution)/shard_map/psum | solution.py:37
  76.9 0.9 fusion.5
  77.8 0.4 fusion.3
  78.2 0.8 copy.17
  79.1 0.0 reduce-scatter.8.cloned.1.call-update
  79.1 0.0 reduce-scatter.6.cloned.1.call-start
  79.2 1.1 fusion.7
  80.3 1.0 fusion.1
  81.3 1.7 copy.15
  83.0 0.0 reduce-scatter.6.cloned.1.call-update
  83.0 2.9 %fusion.8 = f32[4,128,2048]{2,1,0:T(8,128)} fusion(bf16[4,16,2048]{2,1,0:T(8,128)(2,1)S(1)} %gather_fusion.1, f32[4,128,16]{1,2,0:T(8,128)S(1)} %copy-done.2), kind=kOutput, calls=%fused_computation.15 | convolution fusion | flops 33570816 | bytes 4489216 | tf_op jit(solution)/shard_map/sqr,srd->sqd/dot_general | solution.py:40
  85.9 119.9 %reduce-scatter.4.cloned.1.call-done = f32[512,2048]{1,0:T(8,128)} async-done(((f32[512,8192]{1,0:T(8,128)}), f32[512,2048]{1,0:T(8,128)}) %reduce-scatter.4.cloned.1.call-update) | async-done | bytes 4194320 | tf_op jit(solution)/shard_map/reduce_scatter | solution.py:49
  205.8 5.4 %fusion = bf16[512,2048]{1,0:T(8,128)(2,1)} fusion(f32[512,2048]{1,0:T(8,128)} %reduce-scatter.4.cloned.1.call-done, f32[4,128,2048]{2,1,0:T(8,128)} %fusion.8), kind=kLoop, calls=%fused_computation.3 | loop fusion | flops 2097152 | bytes 10485760 | tf_op jit(solution)/shard_map/convert_element_type | solution.py:50
  211.2 17.1 %reduce-scatter.8.cloned.1.call-done = f32[2,16,512]{2,1,0:T(8,128)} async-done(((f32[8,16,512]{2,1,0:T(8,128)}), f32[2,16,512]{2,1,0:T(8,128)}) %reduce-scatter.8.cloned.1.call-update) | async-done | bytes 65552 | tf_op jit(solution)/shard_map/reduce_scatter | solution.py:64
  228.3 28.3 %reduce-scatter.6.cloned.1.call-done = f32[2,16,2048]{2,1,0:T(8,128)} async-done(((f32[8,16,2048]{2,1,0:T(8,128)}), f32[2,16,2048]{2,1,0:T(8,128)}) %reduce-scatter.6.cloned.1.call-update) | async-done | bytes 262160 | tf_op jit(solution)/shard_map/reduce_scatter | solution.py:63
  (4 shorter events, 0.0 us)
Async XLA Ops:
  7.2 35.7 %copy-start = (bf16[512,2048]{1,0:T(8,128)(2,1)S(1)}, bf16[512,2048]{1,0:T(8,128)(2,1)}, u32[]{:S(2)}) copy-start(bf16[512,2048]{1,0:T(8,128)(2,1)} %param.7) | copy-start | bytes 6291460
  7.2 37.0 %copy-start.1 = (bf16[512,512]{1,0:T(8,128)(2,1)S(1)}, bf16[512,512]{1,0:T(8,128)(2,1)}, u32[]{:S(2)}) copy-start(bf16[512,512]{1,0:T(8,128)(2,1)} %param.8) | copy-start | bytes 1572868
  7.2 69.7 %all-reduce.3.cloned.1.call-start = ((), (), s32[]{:S(2)}) async-start(), calls=%async_computation.6 | async-start | bytes 131072 | tf_op jit(solution)/shard_map/psum | solution.py:37
  44.1 161.6 %reduce-scatter.4.cloned.1.call-start = ((), (), s32[]{:S(2)}) async-start(), calls=%async_computation.3 | async-start | bytes 20971520 | tf_op jit(solution)/shard_map/reduce_scatter | solution.py:49
  55.8 172.5 %reduce-scatter.8.cloned.1.call-start = ((), (), s32[]{:S(2)}) async-start(), calls=%async_computation.5 | async-start | bytes 327680 | tf_op jit(solution)/shard_map/reduce_scatter | solution.py:64
  77.8 5.2 %copy-start.2 = (f32[4,128,16]{1,2,0:T(8,128)S(1)}, f32[4,128,16]{1,2,0:T(8,128)}, u32[]{:S(2)}) copy-start(f32[4,128,16]{1,2,0:T(8,128)} %get-tuple-element.6) | copy-start | bytes 98308
  79.1 177.4 %reduce-scatter.6.cloned.1.call-start = ((), (), s32[]{:S(2)}) async-start(), calls=%async_computation.4 | async-start | bytes 1310720 | tf_op jit(solution)/shard_map/reduce_scatter | solution.py:63
Sparse Core Ops, SparseCore 0:
  44.3 32.5 all-reduce.2
  79.6 126.1 reduce-scatter.3
  208.6 19.6 reduce-scatter.7
  231.1 25.3 reduce-scatter.5
where the time goes:
time: 263 us
  waiting for transfers between devices  186 us (71%)
  blocking collectives  31.7 us (12%)
  matrix products  21.1 us (8%)
  between operations  13.8 us (5%)
  other arithmetic  6.27 us (2%)
  local copies, waits for them, and re-layouts  3.65 us (1%)
    reduce_scatter x1, waiting for transfers between devices, shards(): lax.psum_scatter(partial_sum, 'tensor', scatter_dimension=1, tiled=True)  120 us
    reduce_scatter x1, waiting for transfers between devices, shards(): lax.psum_scatter(dense_down, 'dp', scatter_dimension=0, tiled=True)  28.3 us
    psum x1, waiting for transfers between devices, shards(): low_rank_input, low_rank_gradient = lax.psum((in_part, grad_part), 'tensor')  21.1 us
    all_gather x1, blocking collectives, shards(): lax.all_gather(adapter_down_weight, 'dp', axis=0, tiled=True)  17.7 us
    reduce_scatter x1, waiting for transfers between devices, shards(): lax.psum_scatter(dense_part, 'dp', scatter_dimension=0, tiled=True)  17.1 us
    all_gather x1, blocking collectives, shards(): lax.all_gather(adapter_up_weight, 'dp', axis=0, tiled=True)  14 us
    dot_general x1, matrix products, shards(): lax.dot_general(key_value_gradient, key_value_weight, (((1,), (1,)), ((),...  11.5 us
    convert_element_type x1, other arithmetic, shards(): grad_input = (base_term + adapter_term).astype(jnp.bfloat16)  5.41 us
  transfers between devices with their start and end apart: 4, of which 4 were waited for; matrix products, arithmetic and copies ran while one was open for 10% of the time, Pallas kernels for 0%

commit v1 on v0

v1 whole, which is shorter than its diff:
```python
import functools

import jax
import jax.numpy as jnp
from jax import lax
from jax.experimental import pallas as pl
from jax.experimental.pallas import tpu as pltpu
from jax.sharding import PartitionSpec as P

SEG = 128
MESH = pl.DeviceIdType.MESH
CHUNK = 256
FIRST = 4

adapter_scale = 2.0

NT = (((1,), (1,)), ((), ()))


def dot(a, b, dims=(((1,), (0,)), ((), ()))):
    return lax.dot_general(a, b, dims, preferred_element_type=jnp.float32)


def kernel(
    dp,
    rank,
    seg_ref,
    slot_ref,
    x_hbm,
    g_hbm,
    w_hbm,
    down_hbm,
    up_hbm,
    out_hbm,
    grad_down_hbm,
    grad_up_hbm,
    x,
    g,
    w_far,
    w_own,
    down,
    up,
    send,
    recv,
    acc,
    out,
    prod_in,
    prod_grad,
    low,
    low_mate,
    low_pair,
    low_peer,
    wide_grad,
    wide_in,
    rows_grad,
    dense_down,
    dense_up,
    send_down,
    send_up,
    recv_down,
    recv_up,
    final_down,
    final_up,
    load_sem,
    out_sem,
    g_send,
    g_recv,
    far_send,
    far_recv,
    own_send,
    own_recv,
    map_send,
    map_recv,
    low_send,
    low_recv,
    chunk_send,
    chunk_recv,
    term_send,
    term_recv,
):
    t = lax.axis_index("tensor")
    me = lax.axis_index("dp")
    mate = t + 1 - 2 * lax.rem(t, 2)
    peer = lax.rem(t + 2, 4)
    cross = 3 - t
    rows, feats = x.shape
    chunks = feats // CHUNK
    segs = rows // SEG
    held = down.shape[0] // dp
    slots = down.shape[0] // rank
    blocks = down.shape[0] // 128

    def local(src, dst, sem):
        return pltpu.make_async_copy(src, dst, sem)

    def remote(src, dst, send_sem, recv_sem, **where):
        return pltpu.make_async_remote_copy(
            src_ref=src, dst_ref=dst, send_sem=send_sem, recv_sem=recv_sem, device_id=where, device_id_type=MESH
        )

    def held_rows(ref, index):
        return ref.at[pl.ds(pl.multiple_of(index * held, held), held)]

    def chunk_rows(ref, base, k):
        return ref.at[pl.ds(pl.multiple_of(base * feats + k * CHUNK, CHUNK), CHUNK)]

    loads = [
        local(g_hbm, g.at[0], load_sem.at[0]),
        local(w_hbm.at[pl.ds(pl.multiple_of(peer * feats, feats), feats)], w_far.at[0], load_sem.at[1]),
        local(x_hbm, x, load_sem.at[2]),
        local(down_hbm, held_rows(down, me), load_sem.at[3]),
        local(up_hbm, held_rows(up, me), load_sem.at[4]),
        local(w_hbm.at[pl.ds(pl.multiple_of(t * feats, feats), feats)], w_own.at[0], load_sem.at[5]),
    ]
    for load in loads:
        load.start()

    barrier = pltpu.get_barrier_semaphore()
    pl.semaphore_signal(barrier, inc=1, device_id={"tensor": mate}, device_id_type=MESH)
    pl.semaphore_signal(barrier, inc=1, device_id={"tensor": peer}, device_id_type=MESH)
    for d in range(1, dp):
        pl.semaphore_signal(barrier, inc=1, device_id={"dp": lax.rem(me + d, dp)}, device_id_type=MESH)
    pl.semaphore_wait(barrier, dp + 1)

    copy_g = remote(g_hbm, g.at[1], g_send, g_recv, tensor=mate)
    copy_g.start()

    def copy_far(k):
        return remote(
            chunk_rows(w_hbm, cross, k), chunk_rows(w_far.at[1], 0, k), far_send.at[k], far_recv.at[k], tensor=mate
        )

    for k in range(chunks):
        copy_far(k).start()
    maps = []
    for d in range(1, dp):
        target = lax.rem(me + d, dp)
        maps.append(remote(up_hbm, held_rows(up, me), map_send.at[0, d], map_recv.at[0, d], dp=target))
        maps.append(remote(down_hbm, held_rows(down, me), map_send.at[1, d], map_recv.at[1, d], dp=target))
    for copy in maps:
        copy.start()
    copy_own = remote(
        w_hbm.at[pl.ds(pl.multiple_of(mate * feats, feats), feats)], w_own.at[1], own_send, own_recv, tensor=mate
    )
    copy_own.start()

    def copy_chunk(k):
        return remote(send.at[k], recv.at[k], chunk_send.at[k], chunk_recv.at[k], tensor=peer)

    def send_chunk(k, carry):
        copy_far(k).wait_recv()
        at = pl.ds(pl.multiple_of(k * CHUNK, CHUNK), CHUNK)
        part = dot(g[0], w_far[0, at, :], NT) + dot(g[1], w_far[1, at, :], NT)
        send[k] = part.astype(jnp.bfloat16)
        copy_chunk(k).start()
        return carry

    loads[0].wait()
    loads[1].wait()
    copy_g.wait_recv()
    lax.fori_loop(0, FIRST, send_chunk, 0)

    for load in loads[2:5]:
        load.wait()
    for copy in maps:
        copy.wait_recv()

    def project(b, carry):
        at = pl.ds(pl.multiple_of(b * 128, 128), 128)
        prod_in[at, :] = dot(down[at, :], x[...], NT)
        prod_grad[at, :] = dot(up[at, :], g[0], NT)
        return carry

    lax.fori_loop(0, blocks, project, 0)
    chosen = []
    for s in range(segs):
        adapter = jnp.full((rank, SEG), seg_ref[s], jnp.int32)
        slot = jnp.zeros((rank, SEG), jnp.int32)
        for j in range(slots):
            slot = jnp.where(adapter == j, jnp.full((rank, SEG), slot_ref[j], jnp.int32), slot)
        chosen.append(slot)
    low[...] = jnp.zeros_like(low)

    def select(a, carry):
        at = pl.ds(pl.multiple_of(a * rank, rank), rank)
        for s in range(segs):
            span = slice(s * SEG, (s + 1) * SEG)
            low[0:rank, span] = jnp.where(chosen[s] == a, prod_in[at, span], low[0:rank, span])
            low[rank : 2 * rank, span] = jnp.where(chosen[s] == a, prod_grad[at, span], low[rank : 2 * rank, span])
        return carry

    lax.fori_loop(0, slots, select, 0)
    copy_low = remote(low, low_mate, low_send.at[0], low_recv.at[0], tensor=mate)
    copy_low.start()
    copy_low.wait_recv()
    low_pair[...] = low[...] + low_mate[...]
    copy_pair = remote(low_pair, low_peer, low_send.at[1], low_recv.at[1], tensor=peer)
    copy_pair.start()

    lax.fori_loop(FIRST, chunks, send_chunk, 0)

    loads[5].wait()
    copy_own.wait_recv()

    def own_chunk(k, carry):
        at = pl.ds(pl.multiple_of(k * CHUNK, CHUNK), CHUNK)
        acc[k] = dot(g[0], w_own[0, at, :], NT) + dot(g[1], w_own[1, at, :], NT)
        return carry

    lax.fori_loop(0, chunks, own_chunk, 0)

    copy_pair.wait_recv()
    scaled = (adapter_scale * (low_pair[...] + low_peer[...])).astype(jnp.bfloat16).astype(jnp.float32)

    def widen(a, carry):
        at = pl.ds(pl.multiple_of(a * rank, rank), rank)
        for s in range(segs):
            span = slice(s * SEG, (s + 1) * SEG)
            wide_in[at, span] = jnp.where(chosen[s] == a, scaled[0:rank, span], 0.0)
            wide_grad[at, span] = jnp.where(chosen[s] == a, scaled[rank : 2 * rank, span], 0.0)
        return carry

    lax.fori_loop(0, slots, widen, 0)

    def terms(b, carry):
        at = pl.ds(pl.multiple_of(b * 128, 128), 128)
        left = wide_grad[at, :].astype(jnp.bfloat16)
        for n in range(feats // 512):
            span = slice(n * 512, (n + 1) * 512)
            value = dot(left, x[:, span])
            dense_down[at, span] = value
            send_down[at, span] = value.astype(jnp.bfloat16)
        value = dot(wide_in[at, :].astype(jnp.bfloat16), g[0])
        dense_up[at, :] = value
        send_up[at, :] = value.astype(jnp.bfloat16)
        return carry

    lax.fori_loop(0, blocks, terms, 0)
    copies = []
    for d in range(1, dp):
        target = lax.rem(me + d, dp)
        copies.append(
            remote(held_rows(send_down, target), recv_down.at[d], term_send.at[0, d], term_recv.at[0, d], dp=target)
        )
        copies.append(
            remote(held_rows(send_up, target), recv_up.at[d], term_send.at[1, d], term_recv.at[1, d], dp=target)
        )
    for copy in copies:
        copy.start()

    for b in range(blocks):
        span = slice(b * 128, (b + 1) * 128)
        rows_grad[:, span] = wide_grad[span, :].T.astype(jnp.bfloat16)

    for k in range(chunks):
        acc[k] = acc[k] + dot(rows_grad[...], down[:, k * CHUNK : (k + 1) * CHUNK])

    outs = []
    for k in range(chunks):
        copy_chunk(k).wait_recv()
        out[k] = (acc[k] + recv[k].astype(jnp.float32)).astype(jnp.bfloat16)
        outs.append(local(out.at[k], out_hbm.at[:, pl.ds(k * CHUNK, CHUNK)], out_sem.at[k]))
        outs[k].start()

    for copy in copies:
        copy.wait_recv()
    mine = pl.ds(pl.multiple_of(me * held, held), held)
    final_down[...] = dense_down[mine, :]
    final_up[...] = dense_up[mine, :]
    for d in range(1, dp):
        final_down[...] += recv_down[d].astype(jnp.float32)
        final_up[...] += recv_up[d].astype(jnp.float32)
    outs.append(local(final_down, grad_down_hbm, out_sem.at[chunks]))
    outs.append(local(final_up, grad_up_hbm, out_sem.at[chunks + 1]))
    outs[chunks].start()
    outs[chunks + 1].start()

    copy_g.wait_send()
    copy_own.wait_send()
    copy_low.wait_send()
    copy_pair.wait_send()
    for k in range(chunks):
        copy_far(k).wait_send()
        copy_chunk(k).wait_send()
    for copy in maps + copies:
        copy.wait_send()
    for copy in outs:
        copy.wait()


def shards(
    dp,
    normed_layer_input,
    key_value_gradient,
    key_value_weight,
    adapter_down_weight,
    adapter_up_weight,
    segment_adapter,
    slot_per_adapter,
):
    rows, feats = normed_layer_input.shape
    cols = key_value_gradient.shape[1]
    count, rank, _ = adapter_down_weight.shape
    held = count * rank
    wide = dp * held
    chunks = feats // CHUNK
    bf16, f32 = jnp.bfloat16, jnp.float32
    vmem, dma = pltpu.VMEM, pltpu.SemaphoreType.DMA
    anywhere = pl.BlockSpec(memory_space=pl.ANY)
    smem = pl.BlockSpec(memory_space=pltpu.SMEM)
    grad_input, grad_down, grad_up = pl.pallas_call(
        functools.partial(kernel, dp, rank),
        out_shape=(
            jax.ShapeDtypeStruct((rows, feats), bf16),
            jax.ShapeDtypeStruct((held, feats), f32),
            jax.ShapeDtypeStruct((held, cols), f32),
        ),
        in_specs=[smem, smem] + [anywhere] * 5,
        out_specs=(anywhere,) * 3,
        scratch_shapes=[
            vmem((rows, feats), bf16),
            vmem((2, rows, cols), bf16),
            vmem((2, feats, cols), bf16),
            vmem((2, feats, cols), bf16),
            vmem((wide, feats), bf16),
            vmem((wide, cols), bf16),
            vmem((chunks, rows, CHUNK), bf16),
            vmem((chunks, rows, CHUNK), bf16),
            vmem((chunks, rows, CHUNK), f32),
            vmem((chunks, rows, CHUNK), bf16),
            vmem((wide, rows), f32),
            vmem((wide, rows), f32),
            vmem((2 * rank, rows), f32),
            vmem((2 * rank, rows), f32),
            vmem((2 * rank, rows), f32),
            vmem((2 * rank, rows), f32),
            vmem((wide, rows), f32),
            vmem((wide, rows), f32),
            vmem((rows, wide), bf16),
            vmem((wide, feats), f32),
            vmem((wide, cols), f32),
            vmem((wide, feats), bf16),
            vmem((wide, cols), bf16),
            vmem((dp, held, feats), bf16),
            vmem((dp, held, cols), bf16),
            vmem((held, feats), f32),
            vmem((held, cols), f32),
            dma((6,)),
            dma((chunks + 2,)),
            dma,
            dma,
            dma((chunks,)),
            dma((chunks,)),
            dma,
            dma,
            dma((2, dp)),
            dma((2, dp)),
            dma((2,)),
            dma((2,)),
            dma((chunks,)),
            dma((chunks,)),
            dma((2, dp)),
            dma((2, dp)),
        ],
        compiler_params=pltpu.CompilerParams(
            collective_id=0, has_side_effects=True, vmem_limit_bytes=60 * 1024 * 1024
        ),
    )(
        segment_adapter,
        slot_per_adapter,
        normed_layer_input,
        key_value_gradient,
        key_value_weight,
        adapter_down_weight.reshape(held, feats),
        adapter_up_weight.reshape(held, cols),
    )
    return grad_input, grad_down.reshape(count, rank, feats), grad_up.reshape(count, rank, cols)


def solution(mesh):
    placed = (
        P(("groups", "dp"), "tensor"),
        P(("groups", "dp"), "tensor"),
        P(None, "tensor"),
        P("dp", None, "tensor"),
        P("dp", None, "tensor"),
        P(("groups", "dp")),
        P(),
    )
    return jax.shard_map(
        functools.partial(shards, mesh.shape["dp"]),
        mesh=mesh,
        in_specs=placed,
        out_specs=(
            P(("groups", "dp"), "tensor"),
            P(("groups", "dp"), None, "tensor"),
            P(("groups", "dp"), None, "tensor"),
        ),
        check_vma=False,
    )
```

time: 263 us -> 64 us (0.24)
  waiting for transfers between devices: 186 us -> 0 us
  Pallas kernels: 0 us -> 58.6 us
  blocking collectives: 31.7 us -> 0 us
  matrix products: 21.1 us -> 0 us
  between operations: 13.8 us -> 0.66 us
  other arithmetic: 6.27 us -> 0 us
    reduce_scatter x3 -> x0, waiting for transfers between devices: 165 us -> none  [the longest x1 120 us: shards(): lax.psum_scatter(partial_sum, 'tensor', scatter_dimension=1, tiled=True)]
    pallas_call x0 -> x1, Pallas kernels: none -> 58.6 us  [shards(): pl.pallas_call(functools.partial(kernel, dp, rank), out_shape=(jax.ShapeD...]
    all_gather x2 -> x0, blocking collectives: 31.7 us -> none  [the longest x1 17.7 us: shards(): lax.all_gather(adapter_down_weight, 'dp', axis=0, tiled=True)]
    dot_general x8 -> x0, matrix products: 21.1 us -> none  [the longest x1 11.5 us: shards(): lax.dot_general(key_value_gradient, key_value_weight, (((1,), (1,)), ((),...]
    psum x1 -> x0, waiting for transfers between devices: 21.1 us -> none  [shards(): low_rank_input, low_rank_gradient = lax.psum((in_part, grad_part), 'tensor')]
    convert_element_type x1 -> x0, other arithmetic: 5.41 us -> none  [shards(): grad_input = (base_term + adapter_term).astype(jnp.bfloat16)]
    unnamed x6 -> x7, local copies, waits for them, and re-layouts: 0.02 us -> 4.54 us
  transfers between devices with their start and end apart: 4 -> 0, of which waited for: 4 -> 0; matrix products, arithmetic and copies ran while one was open for 10% -> 0% of each run, Pallas kernels for 0% -> 0%
where the time goes in v1:
time: 64 us; the launch traced here: 63.8 us
  Pallas kernels  58.6 us (92%)
  local copies, waits for them, and re-layouts  4.54 us (7%)
  between operations  0.66 us (1%)
    pallas_call x1, Pallas kernels, shards(): pl.pallas_call(functools.partial(kernel, dp, rank), out_shape=(jax.ShapeD...  58.6 us
    unnamed x7, local copies, waits for them, and re-layouts  4.54 us

profile of v1, /device:TPU:0, one launch (start us, length us, event | category | flops | bytes accessed | tf_op | source)
XLA Modules:
  0.0 63.8 jit_solution(9625446189489190506)
XLA Ops:
  0.6 58.6 %shard_map.94 = (bf16[512,2048]{1,0:T(8,128)(2,1)}, f32[32,2048]{1,0:T(8,128)}, f32[32,512]{1,0:T(8,128)}) custom-call(s32[4]{0:T(128)} %seg_ref.1, s32[8]{0:T(128)} %slot_ref.1, bf16[512,2048]{1,0:T(8,128)(2,1)} %x_hbm.1, bf16[512,512]{1,0:T(8,128)(2,1)} %g_hbm.1, bf16[8192,512]{1,0:T(8,128)(2,1)} %w_hbm.1, bf16[32,2048]{1,0:T(8,128)(2,1)} %bitcast.5, ...), custom_call_target="tpu_custom_call" | custom-call | tf_op jit(solution)/shard_map/pallas_call | solution.py:311
  59.2 0.0 copy-start
  59.2 0.0 copy-start.1
  59.2 3.2 %copy.13 = bf16[512,2048]{1,0:T(8,128)(2,1)} copy(bf16[512,2048]{1,0:T(8,128)(2,1)} %get-tuple-element.12) | data formatting | bytes 4194304
  62.5 0.0 copy-done
  62.5 0.7 %copy.14 = f32[2,16,2048]{2,1,0:T(8,128)} copy(f32[2,16,2048]{2,1,0:T(8,128)S(1)} %bitcast.4) | data formatting | bytes 524288
  63.2 0.0 copy-done.1
  63.2 0.6 copy.15
Async XLA Ops:
  59.2 3.2 %copy-start = (f32[32,2048]{1,0:T(8,128)S(1)}, f32[32,2048]{1,0:T(8,128)}, u32[]{:S(2)}) copy-start(f32[32,2048]{1,0:T(8,128)} %get-tuple-element.7) | copy-start | bytes 786436
  59.2 3.9 %copy-start.1 = (f32[32,512]{1,0:T(8,128)S(1)}, f32[32,512]{1,0:T(8,128)}, u32[]{:S(2)}) copy-start(f32[32,512]{1,0:T(8,128)} %get-tuple-element.8) | copy-start | bytes 196612

commit v2 on v1

--- a/solution.py
+++ b/solution.py
@@ -31,9 +31,9 @@
     w_hbm,
     down_hbm,
     up_hbm,
-    out_hbm,
-    grad_down_hbm,
-    grad_up_hbm,
+    out,
+    final_down,
+    final_up,
     x,
     g,
     w_far,
@@ -43,7 +43,6 @@
     send,
     recv,
     acc,
-    out,
     prod_in,
     prod_grad,
     low,
@@ -59,10 +58,7 @@
     send_up,
     recv_down,
     recv_up,
-    final_down,
-    final_up,
     load_sem,
-    out_sem,
     g_send,
     g_recv,
     far_send,
@@ -194,7 +190,8 @@
     copy_low.start()
     copy_low.wait_recv()
     low_pair[...] = low[...] + low_mate[...]
-    copy_pair = remote(low_pair, low_peer, low_send.at[1], low_recv.at[1], tensor=peer)
+    half = pl.ds(pl.multiple_of(lax.rem(t, 2) * rank, rank), rank)
+    copy_pair = remote(low_pair.at[half], low_peer.at[half], low_send.at[1], low_recv.at[1], tensor=peer)
     copy_pair.start()
 
     lax.fori_loop(FIRST, chunks, send_chunk, 0)
@@ -210,6 +207,9 @@
     lax.fori_loop(0, chunks, own_chunk, 0)
 
     copy_pair.wait_recv()
+    copy_half = remote(low_peer.at[half], low_peer.at[half], low_send.at[2], low_recv.at[2], tensor=mate)
+    copy_half.start()
+    copy_half.wait_recv()
     scaled = (adapter_scale * (low_pair[...] + low_peer[...])).astype(jnp.bfloat16).astype(jnp.float32)
 
     def widen(a, carry):
@@ -255,12 +255,12 @@
     for k in range(chunks):
         acc[k] = acc[k] + dot(rows_grad[...], down[:, k * CHUNK : (k + 1) * CHUNK])
 
-    outs = []
-    for k in range(chunks):
+    def finish(k):
         copy_chunk(k).wait_recv()
-        out[k] = (acc[k] + recv[k].astype(jnp.float32)).astype(jnp.bfloat16)
-        outs.append(local(out.at[k], out_hbm.at[:, pl.ds(k * CHUNK, CHUNK)], out_sem.at[k]))
-        outs[k].start()
+        out[:, k * CHUNK : (k + 1) * CHUNK] = (acc[k] + recv[k].astype(jnp.float32)).astype(jnp.bfloat16)
+
+    for k in range(chunks - 1):
+        finish(k)
 
     for copy in copies:
         copy.wait_recv()
@@ -270,21 +270,30 @@
     for d in range(1, dp):
         final_down[...] += recv_down[d].astype(jnp.float32)
         final_up[...] += recv_up[d].astype(jnp.float32)
-    outs.append(local(final_down, grad_down_hbm, out_sem.at[chunks]))
-    outs.append(local(final_up, grad_up_hbm, out_sem.at[chunks + 1]))
-    outs[chunks].start()
-    outs[chunks + 1].start()
 
     copy_g.wait_send()
     copy_own.wait_send()
     copy_low.wait_send()
     copy_pair.wait_send()
+    copy_half.wait_send()
     for k in range(chunks):
         copy_far(k).wait_send()
+    for k in range(chunks):
         copy_chunk(k).wait_send()
     for copy in maps + copies:
         copy.wait_send()
-    for copy in outs:
+    finish(chunks - 1)
+
+
+def write(out, grad_down, grad_up, out_hbm, grad_down_hbm, grad_up_hbm, sem):
+    copies = [
+        pltpu.make_async_copy(out, out_hbm, sem.at[0]),
+        pltpu.make_async_copy(grad_down, grad_down_hbm, sem.at[1]),
+        pltpu.make_async_copy(grad_up, grad_up_hbm, sem.at[2]),
+    ]
+    for copy in copies:
+        copy.start()
+    for copy in copies:
         copy.wait()
 
 
@@ -308,15 +317,12 @@
     vmem, dma = pltpu.VMEM, pltpu.SemaphoreType.DMA
     anywhere = pl.BlockSpec(memory_space=pl.ANY)
     smem = pl.BlockSpec(memory_space=pltpu.SMEM)
-    grad_input, grad_down, grad_up = pl.pallas_call(
+    inside = pl.BlockSpec(memory_space=pltpu.VMEM)
+    made = pl.pallas_call(
         functools.partial(kernel, dp, rank),
-        out_shape=(
-            jax.ShapeDtypeStruct((rows, feats), bf16),
-            jax.ShapeDtypeStruct((held, feats), f32),
-            jax.ShapeDtypeStruct((held, cols), f32),
-        ),
+        out_shape=(vmem((rows, feats), bf16), vmem((held, feats), f32), vmem((held, cols), f32)),
         in_specs=[smem, smem] + [anywhere] * 5,
-        out_specs=(anywhere,) * 3,
+        out_specs=(inside,) * 3,
         scratch_shapes=[
             vmem((rows, feats), bf16),
             vmem((2, rows, cols), bf16),
@@ -327,7 +333,6 @@
             vmem((chunks, rows, CHUNK), bf16),
             vmem((chunks, rows, CHUNK), bf16),
             vmem((chunks, rows, CHUNK), f32),
-            vmem((chunks, rows, CHUNK), bf16),
             vmem((wide, rows), f32),
             vmem((wide, rows), f32),
             vmem((2 * rank, rows), f32),
@@ -343,10 +348,7 @@
             vmem((wide, cols), bf16),
             vmem((dp, held, feats), bf16),
             vmem((dp, held, cols), bf16),
-            vmem((held, feats), f32),
-            vmem((held, cols), f32),
             dma((6,)),
-            dma((chunks + 2,)),
             dma,
             dma,
             dma((chunks,)),
@@ -355,8 +357,8 @@
             dma,
             dma((2, dp)),
             dma((2, dp)),
-            dma((2,)),
-            dma((2,)),
+            dma((3,)),
+            dma((3,)),
             dma((chunks,)),
             dma((chunks,)),
             dma((2, dp)),
@@ -374,6 +376,17 @@
         adapter_down_weight.reshape(held, feats),
         adapter_up_weight.reshape(held, cols),
     )
+    grad_input, grad_down, grad_up = pl.pallas_call(
+        write,
+        out_shape=(
+            jax.ShapeDtypeStruct((rows, feats), bf16),
+            jax.ShapeDtypeStruct((held, feats), f32),
+            jax.ShapeDtypeStruct((held, cols), f32),
+        ),
+        in_specs=[inside] * 3,
+        out_specs=(anywhere,) * 3,
+        scratch_shapes=[dma((3,))],
+    )(*made)
     return grad_input, grad_down.reshape(count, rank, feats), grad_up.reshape(count, rank, cols)
 
 

time: 64 us -> 63.6 us (level)
  local copies, waits for them, and re-layouts: 4.54 us -> 2.66 us
  Pallas kernels: 58.6 us -> 60.1 us
    unnamed x7 -> x6, local copies, waits for them, and re-layouts: 4.54 us -> 2.66 us
    pallas_call x1 -> x2, Pallas kernels: 58.6 us -> 60.1 us  [the longest x1 57 us: shards(): pl.pallas_call(functools.partial(kernel, dp, rank), out_shape=(vmem((rows...]
where the time goes in v2:
time: 63.6 us; the launch traced here: 63.4 us
  Pallas kernels  60.1 us (94%)
  local copies, waits for them, and re-layouts  2.66 us (4%)
  between operations  0.65 us (1%)
    pallas_call x1, Pallas kernels, shards(): pl.pallas_call(functools.partial(kernel, dp, rank), out_shape=(vmem((rows...  57 us
    pallas_call x1, Pallas kernels, shards(): pl.pallas_call(write, out_shape=(jax.ShapeDtypeStruct((rows, feats), bf16...  3.12 us
    unnamed x6, local copies, waits for them, and re-layouts  2.66 us

profile of v2, /device:TPU:0, one launch (start us, length us, event | category | flops | bytes accessed | tf_op | source)
XLA Modules:
  0.0 63.4 jit_solution(9733580282582329924)
XLA Ops:
  0.6 57.0 %shard_map.94 = (bf16[512,2048]{1,0:T(8,128)(2,1)S(1)}, f32[32,2048]{1,0:T(8,128)S(1)}, f32[32,512]{1,0:T(8,128)S(1)}) custom-call(s32[4]{0:T(128)} %seg_ref.1, s32[8]{0:T(128)} %slot_ref.1, bf16[512,2048]{1,0:T(8,128)(2,1)} %x_hbm.1, bf16[512,512]{1,0:T(8,128)(2,1)} %g_hbm.1, bf16[8192,512]{1,0:T(8,128)(2,1)} %w_hbm.1, bf16[32,2048]{1,0:T(8,128)(2,1)} %bitcast.4, ...), custom_call_target="tpu_custom_call" | custom-call | tf_op jit(solution)/shard_map/pallas_call | solution.py:321
  57.6 0.0 copy-start
  57.6 1.3 %copy-done = bf16[512,2048]{1,0:T(8,128)(2,1)} copy-done((bf16[512,2048]{1,0:T(8,128)(2,1)}, bf16[512,2048]{1,0:T(8,128)(2,1)S(1)}, u32[]{:S(2)}) %copy-start) | copy-done | bytes 2097176
  58.9 0.0 copy-start.1
  58.9 0.7 %copy-done.1 = f32[32,2048]{1,0:T(8,128)} copy-done((f32[32,2048]{1,0:T(8,128)}, f32[32,2048]{1,0:T(8,128)S(1)}, u32[]{:S(2)}) %copy-start.1) | copy-done | bytes 262168
  59.6 0.0 copy-start.2
  59.6 0.6 copy-done.2
  60.3 3.1 %shard_map.95 = (bf16[512,2048]{1,0:T(8,128)(2,1)}, f32[32,2048]{1,0:T(8,128)}, f32[32,512]{1,0:T(8,128)}) custom-call(bf16[512,2048]{1,0:T(8,128)(2,1)} %copy-done, f32[32,2048]{1,0:T(8,128)} %copy-done.1, f32[32,512]{1,0:T(8,128)} %copy-done.2), custom_call_target="tpu_custom_call" | custom-call | tf_op jit(solution)/shard_map/pallas_call | solution.py:379
Async XLA Ops:
  57.6 1.3 %copy-start = (bf16[512,2048]{1,0:T(8,128)(2,1)}, bf16[512,2048]{1,0:T(8,128)(2,1)S(1)}, u32[]{:S(2)}) copy-start(bf16[512,2048]{1,0:T(8,128)(2,1)S(1)} %get-tuple-element.9.out) | copy-start | bytes 6291460
  58.9 0.7 %copy-start.1 = (f32[32,2048]{1,0:T(8,128)}, f32[32,2048]{1,0:T(8,128)S(1)}, u32[]{:S(2)}) copy-start(f32[32,2048]{1,0:T(8,128)S(1)} %get-tuple-element.10.grad_down) | copy-start | bytes 786436
  59.6 0.6 copy-start.2

commit v3 on v2

--- a/solution.py
+++ b/solution.py
@@ -1,4 +1,5 @@
 import functools
+import math
 
 import jax
 import jax.numpy as jnp
@@ -24,8 +25,8 @@
 def kernel(
     dp,
     rank,
-    seg_ref,
-    slot_ref,
+    seg_hbm,
+    slot_hbm,
     x_hbm,
     g_hbm,
     w_hbm,
@@ -58,6 +59,8 @@
     send_up,
     recv_down,
     recv_up,
+    seg_ref,
+    slot_ref,
     load_sem,
     g_send,
     g_recv,
@@ -107,6 +110,8 @@
         local(down_hbm, held_rows(down, me), load_sem.at[3]),
         local(up_hbm, held_rows(up, me), load_sem.at[4]),
         local(w_hbm.at[pl.ds(pl.multiple_of(t * feats, feats), feats)], w_own.at[0], load_sem.at[5]),
+        local(seg_hbm, seg_ref, load_sem.at[6]),
+        local(slot_hbm, slot_ref, load_sem.at[7]),
     ]
     for load in loads:
         load.start()
@@ -156,7 +161,7 @@
     copy_g.wait_recv()
     lax.fori_loop(0, FIRST, send_chunk, 0)
 
-    for load in loads[2:5]:
+    for load in loads[2:5] + loads[6:8]:
         load.wait()
     for copy in maps:
         copy.wait_recv()
@@ -316,39 +321,44 @@
     bf16, f32 = jnp.bfloat16, jnp.float32
     vmem, dma = pltpu.VMEM, pltpu.SemaphoreType.DMA
     anywhere = pl.BlockSpec(memory_space=pl.ANY)
-    smem = pl.BlockSpec(memory_space=pltpu.SMEM)
+    buffers = [
+        vmem((rows, feats), bf16),
+        vmem((2, rows, cols), bf16),
+        vmem((2, feats, cols), bf16),
+        vmem((2, feats, cols), bf16),
+        vmem((wide, feats), bf16),
+        vmem((wide, cols), bf16),
+        vmem((chunks, rows, CHUNK), bf16),
+        vmem((chunks, rows, CHUNK), bf16),
+        vmem((chunks, rows, CHUNK), f32),
+        vmem((wide, rows), f32),
+        vmem((wide, rows), f32),
+        vmem((2 * rank, rows), f32),
+        vmem((2 * rank, rows), f32),
+        vmem((2 * rank, rows), f32),
+        vmem((2 * rank, rows), f32),
+        vmem((wide, rows), f32),
+        vmem((wide, rows), f32),
+        vmem((rows, wide), bf16),
+        vmem((wide, feats), f32),
+        vmem((wide, cols), f32),
+        vmem((wide, feats), bf16),
+        vmem((wide, cols), bf16),
+        vmem((dp, held, feats), bf16),
+        vmem((dp, held, cols), bf16),
+    ]
+    used = sum(math.prod(buffer.shape) * jnp.dtype(buffer.dtype).itemsize for buffer in buffers)
     inside = pl.BlockSpec(memory_space=pltpu.VMEM)
     made = pl.pallas_call(
         functools.partial(kernel, dp, rank),
         out_shape=(vmem((rows, feats), bf16), vmem((held, feats), f32), vmem((held, cols), f32)),
-        in_specs=[smem, smem] + [anywhere] * 5,
+        in_specs=[anywhere] * 7,
         out_specs=(inside,) * 3,
-        scratch_shapes=[
-            vmem((rows, feats), bf16),
-            vmem((2, rows, cols), bf16),
-            vmem((2, feats, cols), bf16),
-            vmem((2, feats, cols), bf16),
-            vmem((wide, feats), bf16),
-            vmem((wide, cols), bf16),
-            vmem((chunks, rows, CHUNK), bf16),
-            vmem((chunks, rows, CHUNK), bf16),
-            vmem((chunks, rows, CHUNK), f32),
-            vmem((wide, rows), f32),
-            vmem((wide, rows), f32),
-            vmem((2 * rank, rows), f32),
-            vmem((2 * rank, rows), f32),
-            vmem((2 * rank, rows), f32),
-            vmem((2 * rank, rows), f32),
-            vmem((wide, rows), f32),
-            vmem((wide, rows), f32),
-            vmem((rows, wide), bf16),
-            vmem((wide, feats), f32),
-            vmem((wide, cols), f32),
-            vmem((wide, feats), bf16),
-            vmem((wide, cols), bf16),
-            vmem((dp, held, feats), bf16),
-            vmem((dp, held, cols), bf16),
-            dma((6,)),
+        scratch_shapes=buffers
+        + [
+            pltpu.SMEM(segment_adapter.shape, jnp.int32),
+            pltpu.SMEM(slot_per_adapter.shape, jnp.int32),
+            dma((8,)),
             dma,
             dma,
             dma((chunks,)),
@@ -365,16 +375,21 @@
             dma((2, dp)),
         ],
         compiler_params=pltpu.CompilerParams(
-            collective_id=0, has_side_effects=True, vmem_limit_bytes=60 * 1024 * 1024
+            collective_id=0, has_side_effects=True, vmem_limit_bytes=used + 8 * 2**20
         ),
     )(
-        segment_adapter,
-        slot_per_adapter,
-        normed_layer_input,
-        key_value_gradient,
-        key_value_weight,
-        adapter_down_weight.reshape(held, feats),
-        adapter_up_weight.reshape(held, cols),
+        *[
+            pltpu.with_memory_space_constraint(array, pltpu.HBM)
+            for array in (
+                segment_adapter,
+                slot_per_adapter,
+                normed_layer_input,
+                key_value_gradient,
+                key_value_weight,
+                adapter_down_weight.reshape(held, feats),
+                adapter_up_weight.reshape(held, cols),
+            )
+        ],
     )
     grad_input, grad_down, grad_up = pl.pallas_call(
         write,
@@ -386,7 +401,8 @@
         in_specs=[inside] * 3,
         out_specs=(anywhere,) * 3,
         scratch_shapes=[dma((3,))],
-    )(*made)
+        compiler_params=pltpu.CompilerParams(vmem_limit_bytes=2**20),
+    )(*[pltpu.with_memory_space_constraint(array, pltpu.VMEM) for array in made])
     return grad_input, grad_down.reshape(count, rank, feats), grad_up.reshape(count, rank, cols)
 
 

time: 63.6 us -> 58.5 us (0.920)
  local copies, waits for them, and re-layouts: 2.66 us -> 0 us
  Pallas kernels: 60.1 us -> 57.7 us
    unnamed x6 -> x0, local copies, waits for them, and re-layouts: 2.66 us -> none
    pallas_call x1, Pallas kernels: 3.12 us -> 1.43 us  [shards(): pl.pallas_call(write, out_shape=(jax.ShapeDtypeStruct((rows, feats), bf16...]
    pallas_call x1, Pallas kernels: 57 us -> 56.3 us  [shards(): pl.pallas_call(functools.partial(kernel, dp, rank), out_shape=(vmem((rows...]
where the time goes in v3:
time: 58.5 us; the launch traced here: 58.4 us
  Pallas kernels  57.7 us (99%)
  between operations  0.64 us (1%)
    pallas_call x1, Pallas kernels, shards(): pl.pallas_call(functools.partial(kernel, dp, rank), out_shape=(vmem((rows...  56.3 us
    pallas_call x1, Pallas kernels, shards(): pl.pallas_call(write, out_shape=(jax.ShapeDtypeStruct((rows, feats), bf16...  1.43 us

profile of v3, /device:TPU:0, one launch (start us, length us, event | category | flops | bytes accessed | tf_op | source)
XLA Modules:
  0.0 58.4 jit_solution(15539989850136756801)
XLA Ops:
  0.6 56.3 %shard_map.94 = (bf16[512,2048]{1,0:T(8,128)(2,1)S(1)}, f32[32,2048]{1,0:T(8,128)S(1)}, f32[32,512]{1,0:T(8,128)S(1)}) custom-call(s32[4]{0:T(128)} %seg_hbm.1, s32[8]{0:T(128)} %slot_hbm.1, bf16[512,2048]{1,0:T(8,128)(2,1)} %x_hbm.1, bf16[512,512]{1,0:T(8,128)(2,1)} %g_hbm.1, bf16[8192,512]{1,0:T(8,128)(2,1)} %w_hbm.1, bf16[32,2048]{1,0:T(8,128)(2,1)} %bitcast.4, ...), custom_call_target="tpu_custom_call" | custom-call | tf_op jit(solution)/shard_map/pallas_call | solution.py:352
  57.0 1.4 %shard_map.95 = (bf16[512,2048]{1,0:T(8,128)(2,1)}, f32[32,2048]{1,0:T(8,128)}, f32[32,512]{1,0:T(8,128)}) custom-call(bf16[512,2048]{1,0:T(8,128)(2,1)S(1)} %get-tuple-element.9.out, f32[32,2048]{1,0:T(8,128)S(1)} %get-tuple-element.10.grad_down, f32[32,512]{1,0:T(8,128)S(1)} %get-tuple-element.11.grad_up), custom_call_target="tpu_custom_call" | custom-call | tf_op jit(solution)/shard_map/pallas_call | solution.py:394

commit v4 on v3

--- a/solution.py
+++ b/solution.py
@@ -11,6 +11,7 @@
 SEG = 128
 MESH = pl.DeviceIdType.MESH
 CHUNK = 256
+EARLY = 2
 FIRST = 4
 
 adapter_scale = 2.0
@@ -76,6 +77,7 @@
     chunk_recv,
     term_send,
     term_recv,
+    ready_sem,
 ):
     t = lax.axis_index("tensor")
     me = lax.axis_index("dp")
@@ -120,8 +122,17 @@
     pl.semaphore_signal(barrier, inc=1, device_id={"tensor": mate}, device_id_type=MESH)
     pl.semaphore_signal(barrier, inc=1, device_id={"tensor": peer}, device_id_type=MESH)
     for d in range(1, dp):
-        pl.semaphore_signal(barrier, inc=1, device_id={"dp": lax.rem(me + d, dp)}, device_id_type=MESH)
-    pl.semaphore_wait(barrier, dp + 1)
+
+        @pl.when(me + d < dp)
+        def _():
+            pl.semaphore_signal(barrier, inc=1, device_id={"dp": lax.rem(me + d, dp)}, device_id_type=MESH)
+
+    pl.semaphore_wait(barrier, me + 2)
+    for d in range(1, dp):
+
+        @pl.when(me >= d)
+        def _():
+            pl.semaphore_signal(ready_sem, inc=1, device_id={"dp": lax.rem(me + dp - d, dp)}, device_id_type=MESH)
 
     copy_g = remote(g_hbm, g.at[1], g_send, g_recv, tensor=mate)
     copy_g.start()
@@ -138,8 +149,6 @@
         target = lax.rem(me + d, dp)
         maps.append(remote(up_hbm, held_rows(up, me), map_send.at[0, d], map_recv.at[0, d], dp=target))
         maps.append(remote(down_hbm, held_rows(down, me), map_send.at[1, d], map_recv.at[1, d], dp=target))
-    for copy in maps:
-        copy.start()
     copy_own = remote(
         w_hbm.at[pl.ds(pl.multiple_of(mate * feats, feats), feats)], w_own.at[1], own_send, own_recv, tensor=mate
     )
@@ -159,9 +168,19 @@
     loads[0].wait()
     loads[1].wait()
     copy_g.wait_recv()
-    lax.fori_loop(0, FIRST, send_chunk, 0)
-
-    for load in loads[2:5] + loads[6:8]:
+    lax.fori_loop(0, EARLY, send_chunk, 0)
+
+    @pl.when(me < dp - 1)
+    def _():
+        pl.semaphore_wait(ready_sem, dp - 1 - me)
+
+    loads[3].wait()
+    loads[4].wait()
+    for copy in maps:
+        copy.start()
+    lax.fori_loop(EARLY, FIRST, send_chunk, 0)
+
+    for load in loads[2:3] + loads[6:8]:
         load.wait()
     for copy in maps:
         copy.wait_recv()
@@ -373,6 +392,7 @@
             dma((chunks,)),
             dma((2, dp)),
             dma((2, dp)),
+            pltpu.SemaphoreType.REGULAR,
         ],
         compiler_params=pltpu.CompilerParams(
             collective_id=0, has_side_effects=True, vmem_limit_bytes=used + 8 * 2**20

time: 58.5 us -> 55.5 us (0.949)
  Pallas kernels: 57.7 us -> 54.7 us
    pallas_call x1, Pallas kernels: 56.3 us -> 53.3 us  [shards(): pl.pallas_call(functools.partial(kernel, dp, rank), out_shape=(vmem((rows...]
where the time goes in v4:
time: 55.5 us; the launch traced here: 55.4 us
  Pallas kernels  54.7 us (99%)
  between operations  0.64 us (1%)
    pallas_call x1, Pallas kernels, shards(): pl.pallas_call(functools.partial(kernel, dp, rank), out_shape=(vmem((rows...  53.3 us
    pallas_call x1, Pallas kernels, shards(): pl.pallas_call(write, out_shape=(jax.ShapeDtypeStruct((rows, feats), bf16...  1.43 us

profile of v4, /device:TPU:0, one launch (start us, length us, event | category | flops | bytes accessed | tf_op | source)
XLA Modules:
  0.0 55.4 jit_solution(14714317070422380247)
XLA Ops:
  0.6 53.3 %shard_map.94 = (bf16[512,2048]{1,0:T(8,128)(2,1)S(1)}, f32[32,2048]{1,0:T(8,128)S(1)}, f32[32,512]{1,0:T(8,128)S(1)}) custom-call(s32[4]{0:T(128)} %seg_hbm.1, s32[8]{0:T(128)} %slot_hbm.1, bf16[512,2048]{1,0:T(8,128)(2,1)} %x_hbm.1, bf16[512,512]{1,0:T(8,128)(2,1)} %g_hbm.1, bf16[8192,512]{1,0:T(8,128)(2,1)} %w_hbm.1, bf16[32,2048]{1,0:T(8,128)(2,1)} %bitcast.4, ...), custom_call_target="tpu_custom_call" | custom-call | tf_op jit(solution)/shard_map/pallas_call | solution.py:371
  53.9 1.4 %shard_map.95 = (bf16[512,2048]{1,0:T(8,128)(2,1)}, f32[32,2048]{1,0:T(8,128)}, f32[32,512]{1,0:T(8,128)}) custom-call(bf16[512,2048]{1,0:T(8,128)(2,1)S(1)} %get-tuple-element.9.out, f32[32,2048]{1,0:T(8,128)S(1)} %get-tuple-element.10.grad_down, f32[32,512]{1,0:T(8,128)S(1)} %get-tuple-element.11.grad_up), custom_call_target="tpu_custom_call" | custom-call | tf_op jit(solution)/shard_map/pallas_call | solution.py:414
